TPU v7x, 256 devices: a whole 4x4x8 slice. The times are simulated.
256 devices in a mesh: ocn: 8 (over z), atm: 32 (over y, x, core).
Axes of the slice: x: 4, y: 4, z: 8, core: 2. Of those that a mesh axis runs over, the one named last changes fastest.
Arguments:
- atm_fields: bfloat16 [2048, 32, 128], P('atm'), may hold values from -6 to 6
- weights: bfloat16 [98304, 128, 128], P(('ocn', 'atm')), may hold values from -0.5 to 0.5
- surf_temp: float32 [98304, 128], P(('ocn', 'atm')), may hold values from -6 to 6
- surf_hum: float32 [98304, 128], P(('ocn', 'atm')), may hold values from -6 to 6
- roughness: float32 [98304, 128], P(('ocn', 'atm')), may hold values from 0.0001 to 0.1
- cell_area: float32 [98304, 128], P(('ocn', 'atm')), may hold values from 0.2 to 2
- need_list: int32 [256, 32, 4], P(('ocn', 'atm')), may hold values from 0 to 63
- use_slot: int32 [98304], P(('ocn', 'atm')), may hold values from 0 to 127, as said below
- ocean_block: int32 [98304], P(('ocn', 'atm')), may hold values from 0 to 31
- ocean_cell: int32 [98304, 128], P(('ocn', 'atm')), may hold values from 0 to 127
- cell_count: int32 [98304], P(('ocn', 'atm')), may hold values from 1 to 128, as said below
- ice_mask: int32 [98304, 128], P(('ocn', 'atm')), may hold values 0 or 1
Outputs:
- atm_flux: float32 [2048, 4, 128], P('atm')
- ocean_flux: float32 [256, 32, 128], P(('ocn', 'atm'))
Inputs may be any that keep to these rules, and one draw needn't show every extreme that they name: `use_slot`: within the 384 exchange blocks of each device every slot value appears at least once. `cell_count`: each device has a block with 128 live cells and one with a single live cell.
All inputs are finite; a program needn't handle non-finite values. No bound on the sum of `ice_mask` on one device may be relied on, other than what follows from the above.
Results may differ from a plain program's by a relative error of at most 0.00087.
Values may be sent and summed in bfloat16 or wider, within the bound.
No kernel may reach another device: no remote copies, remote signals or barrier semaphores. Data moves between devices by JAX's collectives and lax.ppermute only.
A program may use at most 128 MiB of HBM per device.

v0:
```python
import math
import jax
import jax.numpy as jnp
from jax import lax
from jax.sharding import PartitionSpec as P

F = 32
BLK = 128
ACELL = 128
OCELL = 128
CAP = 4
ITERS = 8
OBD = 1
ref_height = 10.0
karman = 0.4
buoyancy = 0.5
flux_scale = 40.0


def similarity(wind_speed, temp_diff, hum_diff, log_mom, log_heat, psi_mom, psi_heat):
    fric_vel = karman * wind_speed / (log_mom - psi_mom)
    temp_scale = karman * temp_diff / (log_heat - psi_heat)
    hum_scale = karman * hum_diff / (log_heat - psi_heat)
    return (fric_vel, temp_scale, hum_scale)


def bulk_fluxes(mapped, surf_temp, surf_hum, roughness, ice_frac):
    wind_u = 6.0 * mapped[:, 0]
    wind_v = 6.0 * mapped[:, 1]
    wind_speed = jnp.sqrt(wind_u * wind_u + wind_v * wind_v + 1.0)
    temp_diff = mapped[:, 2] - surf_temp
    hum_diff = (mapped[:, 3] - surf_hum) * (1.0 - 0.6 * ice_frac)
    log_mom = jnp.log(ref_height / roughness)
    log_heat = log_mom + math.log(10.0)
    psi_mom = jnp.zeros_like(wind_speed)
    psi_heat = jnp.zeros_like(wind_speed)
    for sweep in range(ITERS):
        fric_vel, temp_scale, hum_scale = similarity(
            wind_speed, temp_diff, hum_diff, log_mom, log_heat, psi_mom, psi_heat
        )
        stability = jnp.clip(
            ref_height * karman * buoyancy * (temp_scale + 0.2 * hum_scale) / (fric_vel * fric_vel),
            -5.0,
            1.0,
        )
        unstable = jnp.minimum(stability, 0.0)
        root_term = jnp.sqrt(jnp.sqrt(1.0 - 16.0 * unstable))
        square_term = jnp.log((1.0 + root_term * root_term) / 2.0)
        psi_mom = jnp.where(
            stability >= 0.0,
            -5.0 * stability,
            2.0 * jnp.log((1.0 + root_term) / 2.0)
            + square_term
            - 2.0 * jnp.arctan(root_term)
            + math.pi / 2.0,
        )
        psi_heat = jnp.where(stability >= 0.0, -5.0 * stability, 2.0 * square_term)
    fric_vel, temp_scale, hum_scale = similarity(
        wind_speed, temp_diff, hum_diff, log_mom, log_heat, psi_mom, psi_heat
    )
    return jnp.stack(
        [
            flux_scale * fric_vel * fric_vel * wind_u / wind_speed,
            flux_scale * fric_vel * fric_vel * wind_v / wind_speed,
            -flux_scale * fric_vel * temp_scale,
            -flux_scale * fric_vel * hum_scale,
        ],
        axis=1,
    )


def per_device(
    atm_fields,
    weights,
    surf_temp,
    surf_hum,
    roughness,
    cell_area,
    need_list,
    use_slot,
    ocean_block,
    ocean_cell,
    cell_count,
    ice_mask,
):
    owners = lax.axis_size("atm")
    local_blocks = atm_fields.shape[0]
    slot_total = owners * CAP
    block_total = weights.shape[0]
    wanted = need_list[0]
    requests = lax.all_to_all(wanted, "atm", split_axis=0, concat_axis=0, tiled=True)
    served = atm_fields[requests.reshape(-1)].reshape(owners, CAP, F, ACELL)
    arrived = lax.all_to_all(served, "atm", split_axis=0, concat_axis=0, tiled=True)
    table = arrived.reshape(slot_total, F, ACELL)
    picked = table[use_slot]
    mapped = jnp.einsum("kfa,kba->kfb", picked, weights, preferred_element_type=jnp.float32)
    ice_frac = ice_mask.astype(jnp.float32)
    flux4 = bulk_fluxes(mapped, surf_temp, surf_hum, roughness, ice_frac)
    is_live = (jnp.arange(BLK, dtype=jnp.int32)[None, :] < cell_count[:, None]).astype(jnp.float32)
    cell_weight = cell_area * is_live
    weighted = (cell_weight[:, None, :] * flux4).astype(jnp.bfloat16)
    contrib = jnp.einsum("kcb,kba->kca", weighted, weights, preferred_element_type=jnp.float32)
    slot_hot = (use_slot[:, None] == jnp.arange(slot_total, dtype=jnp.int32)[None, :]).astype(
        jnp.float32
    )
    slot_sums = jnp.dot(
        slot_hot.T, contrib.reshape(block_total, 4 * ACELL), precision=lax.Precision.HIGHEST
    )
    returned = lax.all_to_all(
        slot_sums.reshape(owners, CAP, 4 * ACELL), "atm", split_axis=0, concat_axis=0, tiled=True
    )
    owner_hot = (
        requests.reshape(-1)[:, None] == jnp.arange(local_blocks, dtype=jnp.int32)[None, :]
    ).astype(jnp.float32)
    owner_sums = jnp.dot(
        owner_hot.T, returned.reshape(slot_total, 4 * ACELL), precision=lax.Precision.HIGHEST
    )
    atm_flux = lax.psum(owner_sums, "ocn").reshape(local_blocks, 4, ACELL)
    passive = mapped[:, 4:] * (1.0 - 0.7 * ice_frac)[:, None, :]
    ocean_values = cell_weight[:, None, :] * jnp.concatenate([flux4, passive], axis=1)
    cell_hot = (ocean_cell[:, :, None] == jnp.arange(OCELL, dtype=jnp.int32)[None, None, :]).astype(
        jnp.float32
    )
    partial_sum = jnp.einsum(
        "kfb,kbc->kfc", ocean_values, cell_hot, precision=lax.Precision.HIGHEST
    )
    flat_partial = partial_sum.reshape(block_total, F * OCELL)
    targets = jnp.arange(lax.axis_size("atm") * OBD, dtype=jnp.int32)
    picker = (ocean_block[None, :] == targets[:, None]).astype(jnp.float32)
    ocean_rows = lax.psum_scatter(
        jnp.dot(picker, flat_partial, precision=lax.Precision.HIGHEST),
        "atm",
        scatter_dimension=0,
        tiled=True,
    )
    ocean_flux = ocean_rows.reshape(OBD, F, OCELL)
    return (atm_flux, ocean_flux)


def solution(mesh):
    placed = (
        P("atm", None, None),
        P(("ocn", "atm"), None, None),
        P(("ocn", "atm"), None),
        P(("ocn", "atm"), None),
        P(("ocn", "atm"), None),
        P(("ocn", "atm"), None),
        P(("ocn", "atm"), None, None),
        P(("ocn", "atm")),
        P(("ocn", "atm")),
        P(("ocn", "atm"), None),
        P(("ocn", "atm")),
        P(("ocn", "atm"), None),
    )
    return jax.shard_map(
        per_device,
        mesh=mesh,
        in_specs=placed,
        out_specs=(P("atm", None, None), P(("ocn", "atm"), None, None)),
        check_vma=False,
    )
```

profile of v0, /device:TPU:2, one launch (start us, length us, event | category | flops | bytes accessed | tf_op | source)
XLA Modules:
  0.0 347.1 jit_solution(1982289157801807212)
XLA Ops:
  7.2 0.0 copy-start
  7.2 0.8 copy.35
  8.0 13.6 %all_to_all.19 = s32[32,1,4]{2,1,0:T(1,128)S(1)} all-to-all(s32[32,1,4]{2,1,0:T(1,128)S(1)} %copy.35), channel_id=1, replica_groups=mesh['ocn'=8,'atm'=32] {'atm'}, dimensions={0} | all-to-all | bytes 1024 | tf_op jit(solution)/shard_map/all_to_all | solution.py:91
  21.6 0.1 reshape.90
  21.7 0.0 copy-done
  21.7 1.7 gather_fusion
  23.4 5.0 %all-to-all-start.1 = ((bf16[32,4,32,128]{3,2,1,0:T(8,128)(2,1)}), bf16[32,4,32,128]{3,2,1,0:T(8,128)(2,1)S(1)}, u32[]{:S(2)}, u32[]{:S(2)}) async-start(bf16[32,4,32,128]{3,2,1,0:T(8,128)(2,1)} %bitcast.2), calls=%async_computation.1 | async-start | bytes 2097152 | tf_op jit(solution)/shard_map/all_to_all | solution.py:93
  28.4 0.7 compare_select_fusion
  29.1 1.0 fusion.16
  30.2 14.5 %all-to-all-done.1 = bf16[32,4,32,128]{3,2,1,0:T(8,128)(2,1)S(1)} async-done(((bf16[32,4,32,128]{3,2,1,0:T(8,128)(2,1)}), bf16[32,4,32,128]{3,2,1,0:T(8,128)(2,1)S(1)}, u32[]{:S(2)}, u32[]{:S(2)}) %all-to-all-start.1) | async-done | bytes 1048608 | tf_op jit(solution)/shard_map/all_to_all | solution.py:93
  44.6 3.2 gather_fusion.1
  47.9 14.9 %fusion.27 = f32[384,32,128]{2,1,0:T(8,128)} fusion(bf16[384,32,128]{2,1,0:T(8,128)(2,1)} %gather_fusion.1, bf16[384,128,128]{2,1,0:T(8,128)(2,1)} %param.13), kind=kOutput, calls=%fused_computation.64 | convolution fusion | flops 402653184 | bytes 22020096 | tf_op jit(solution)/shard_map/kfa,kba->kfb/dot_general | solution.py:96
  62.8 4.0 %fusion.26 = (f32[384,1,128]{2,1,0:T(1,128)S(1)}, f32[384,1,128]{2,1,0:T(1,128)S(1)}, f32[384,1,128]{2,1,0:T(1,128)S(1)}, f32[384,1,128]{2,1,0:T(1,128)S(1)}) fusion(f32[384,32,128]{2,1,0:T(8,128)} %fusion.27), kind=kLoop, calls=%fused_computation.63 | loop fusion | bytes 1572864 | tf_op jit(solution)/shard_map/slice | solution.py:31
  66.8 0.0 copy-done.2
  66.8 0.0 copy-done.3
  66.8 0.0 copy-done.4
  66.8 0.0 copy-done.5
  66.8 5.4 %fusion.15 = (f32[384,128]{1,0:T(8,128)S(1)}, f32[384,128]{1,0:T(8,128)S(1)}, f32[384,128]{1,0:T(8,128)S(1)}) fusion(f32[384,1,128]{2,0,1:T(8,128)S(1)} %bitcast.87, f32[384,1,128]{2,0,1:T(8,128)S(1)} %bitcast.85, f32[384,128]{1,0:T(8,128)S(1)} %copy-done.2, s32[384,128]{1,0:T(8,128)S(1)} %copy-done.3, f32[384,128]{1,0:T(8,128)S(1)} %bitcast.89, ...), kind=kLoop, calls=%fused_computation.24 | loop fusion | flops 12337152 | bytes 2162688 | tf_op jit(solution)/shard_map/div | solution.py:63
  72.2 0.4 divide_multiply_fusion.1
  72.6 3.6 %slice_multiply_fusion = f32[384,28,128]{2,1,0:T(8,128)} fusion(f32[384,32,128]{2,1,0:T(8,128)S(1)} %copy-done.1, f32[384,128]{1,0:T(8,128)S(1)} %get-tuple-element.11), kind=kLoop, calls=%fused_computation.8 | loop fusion | flops 1376256 | bytes 11206656 | tf_op jit(solution)/shard_map/mul | solution.py:119
  76.3 30.8 %concatenate.4 = f32[384,32,128]{2,1,0:T(8,128)} concatenate(f32[384,1,128]{2,1,0:T(1,128)S(1)} %bitcast.81, f32[384,1,128]{2,1,0:T(1,128)S(1)} %bitcast.79, f32[384,1,128]{2,1,0:T(1,128)S(1)} %bitcast.75, f32[384,1,128]{2,1,0:T(1,128)S(1)} %bitcast.77, f32[384,28,128]{2,1,0:T(8,128)} %slice_multiply_fusion), dimensions={1} | concatenate | bytes 12582912 | tf_op jit(solution)/shard_map/concatenate | solution.py:120
  107.1 6.4 %fusion.8 = f32[384,4,128]{2,1,0:T(4,128)S(1)} fusion(bf16[384,128,128]{2,1,0:T(8,128)(2,1)} %param.13, f32[384,1,128]{2,1,0:T(1,128)S(1)} %bitcast.78, f32[384,1,128]{2,1,0:T(1,128)S(1)} %bitcast.76, f32[384,1,128]{2,1,0:T(1,128)S(1)} %bitcast.80, f32[384,1,128]{2,1,0:T(1,128)S(1)} %bitcast.82, f32[384,128]{1,0:T(8,128)S(1)} %fusion.16), kind=kOutput, calls=%fused_computation.13 | convolution fusion | flops 51314688 | bytes 14352384 | tf_op jit(solution)/shard_map/kcb,kba->kca/dot_general | solution.py:102
  113.4 0.3 reshape.115
  113.8 0.0 copy-done.7
  113.8 0.5 fusion.17
  114.3 0.9 copy.42
  115.1 5.2 %all-to-all-start.2 = ((f32[32,4,512]{2,1,0:T(4,128)}), f32[32,4,512]{2,1,0:T(4,128)S(1)}, u32[]{:S(2)}, u32[]{:S(2)}) async-start(f32[32,4,512]{2,1,0:T(4,128)} %copy.42), calls=%async_computation.2 | async-start | bytes 524288 | tf_op jit(solution)/shard_map/all_to_all | solution.py:109
  120.3 0.0 copy-start.8
  120.3 0.0 all-reduce.6.cloned.1.call-start
  120.4 20.6 %fusion = f32[384,32,128]{2,1,0:T(8,128)S(1)} fusion(s32[384,128]{1,0:T(8,128)S(1)} %copy-done.6, f32[384,32,128]{2,1,0:T(8,128)} %concatenate.4, f32[384,128]{1,0:T(8,128)S(1)} %fusion.16), kind=kOutput, calls=%fused_computation.3 | convolution fusion | flops 2423783424 | bytes 12976128 | tf_op jit(solution)/shard_map/kfb,kbc->kfc/dot_general | solution.py:124
  141.0 0.0 copy-start.9
  141.0 0.0 copy-done.8
  141.0 6.6 %fusion.2 = f32[32,4096]{1,0:T(8,128)} fusion(f32[48,8,32,128]{3,2,1,0:T(8,128)S(1)} %bitcast.73, s32[384]{0:T(512)S(1)} %copy-done.8), kind=kOutput, calls=%fused_computation.5 | convolution fusion | flops 603992064 | bytes 6817280 | tf_op jit(solution)/shard_map/dot_general | solution.py:131
  147.6 0.0 all-reduce.6.cloned.1.call-update
  147.7 0.0 all-reduce.4.cloned.1.call-start
  147.7 0.6 dynamic-slice
  148.4 0.5 broadcast.204
  148.9 0.7 reduce.5
  149.6 0.1 eq.72
  149.7 0.0 all-to-all-done.2
  149.7 0.1 reshape.94
  149.8 0.3 fusion.21
  150.1 0.7 reshape.95
  150.8 0.0 all-reduce.4.cloned.1.call-update
  150.8 112.9 %all-reduce.6.cloned.1.call-done = f32[32,4096]{1,0:T(8,128)} async-done(((f32[32,4096]{1,0:T(8,128)}), f32[32,4096]{1,0:T(8,128)}) %all-reduce.6.cloned.1.call-update) | async-done | bytes 524304
  263.7 2.2 constant_dynamic-slice_fusion
  265.9 72.8 %all-reduce.4.cloned.1.call-done = f32[64,4,128]{2,1,0:T(4,128)} async-done(((f32[64,4,128]{2,1,0:T(4,128)}), f32[64,4,128]{2,1,0:T(4,128)}) %all-reduce.4.cloned.1.call-update) | async-done | bytes 131088 | tf_op jit(solution)/shard_map/psum | solution.py:118
  338.7 1.6 copy.56
  (14 shorter events, 0.0 us)
Async XLA Ops:
  7.2 14.5 %copy-start = (bf16[64,32,128]{2,1,0:T(8,128)(2,1)S(1)}, bf16[64,32,128]{2,1,0:T(8,128)(2,1)}, u32[]{:S(2)}) copy-start(bf16[64,32,128]{2,1,0:T(8,128)(2,1)} %param.12) | copy-start | bytes 1572868
  23.4 21.3 %all-to-all-start.1 = ((bf16[32,4,32,128]{3,2,1,0:T(8,128)(2,1)}), bf16[32,4,32,128]{3,2,1,0:T(8,128)(2,1)S(1)}, u32[]{:S(2)}, u32[]{:S(2)}) async-start(bf16[32,4,32,128]{3,2,1,0:T(8,128)(2,1)} %bitcast.2), calls=%async_computation.1 | async-start | bytes 2097152 | tf_op jit(solution)/shard_map/all_to_all | solution.py:93
  47.8 18.9 %copy-start.2 = (f32[384,128]{1,0:T(8,128)S(1)}, f32[384,128]{1,0:T(8,128)}, u32[]{:S(2)}) copy-start(f32[384,128]{1,0:T(8,128)} %param.16) | copy-start | bytes 589828
  47.8 18.9 %copy-start.3 = (s32[384,128]{1,0:T(8,128)S(1)}, s32[384,128]{1,0:T(8,128)}, u32[]{:S(2)}) copy-start(s32[384,128]{1,0:T(8,128)} %param.23) | copy-start | bytes 589828
  47.9 18.9 %copy-start.4 = (f32[384,128]{1,0:T(8,128)S(1)}, f32[384,128]{1,0:T(8,128)}, u32[]{:S(2)}) copy-start(f32[384,128]{1,0:T(8,128)} %param.15) | copy-start | bytes 589828
  47.9 18.9 %copy-start.5 = (f32[384,128]{1,0:T(8,128)S(1)}, f32[384,128]{1,0:T(8,128)}, u32[]{:S(2)}) copy-start(f32[384,128]{1,0:T(8,128)} %param.14) | copy-start | bytes 589828
  62.8 9.9 %copy-start.1 = (f32[384,32,128]{2,1,0:T(8,128)S(1)}, f32[384,32,128]{2,1,0:T(8,128)}, u32[]{:S(2)}) copy-start(f32[384,32,128]{2,1,0:T(8,128)} %fusion.27) | copy-start | bytes 18874372
  107.0 6.7 %copy-start.7 = (s32[384]{0:T(512)S(1)}, s32[384]{0:T(512)}, u32[]{:S(2)}) copy-start(s32[384]{0:T(512)} %param.19) | copy-start | bytes 4612
  107.1 13.3 %copy-start.6 = (s32[384,128]{1,0:T(8,128)S(1)}, s32[384,128]{1,0:T(8,128)}, u32[]{:S(2)}) copy-start(s32[384,128]{1,0:T(8,128)} %param.21) | copy-start | bytes 589828
  115.1 34.5 %all-to-all-start.2 = ((f32[32,4,512]{2,1,0:T(4,128)}), f32[32,4,512]{2,1,0:T(4,128)S(1)}, u32[]{:S(2)}, u32[]{:S(2)}) async-start(f32[32,4,512]{2,1,0:T(4,128)} %copy.42), calls=%async_computation.2 | async-start | bytes 524288 | tf_op jit(solution)/shard_map/all_to_all | solution.py:109
  120.3 20.7 %copy-start.8 = (s32[384]{0:T(512)S(1)}, s32[384]{0:T(512)}, u32[]{:S(2)}) copy-start(s32[384]{0:T(512)} %param.20) | copy-start | bytes 4612
  120.3 143.4 %all-reduce.6.cloned.1.call-start = ((), (), s32[]{:S(2)}) async-start(), calls=%async_computation.4 | async-start | bytes 1048576
  141.0 6.7 %copy-start.9 = (u32[256]{0:T(256)S(1)}, u32[256]{0:T(256)}, u32[]{:S(2)}) copy-start(u32[256]{0:T(256)} %constant.72) | copy-start | bytes 3076
  147.7 191.1 %all-reduce.4.cloned.1.call-start = ((), (), s32[]{:S(2)}) async-start(), calls=%async_computation.3 | async-start | bytes 262144 | tf_op jit(solution)/shard_map/psum | solution.py:118
Sparse Core Ops, SparseCore 0:
  147.8 115.9 all-reduce.5
  266.7 71.9 all-reduce.3
where the time goes:
time: 348 us; the launch traced here: 347 us
  waiting for transfers between devices  200 us (57%)
  matrix products  49.3 us (14%)
  local copies, waits for them, and re-layouts  47.6 us (14%)
  between operations  14.3 us (4%)
  blocking collectives  13.6 us (4%)
  other arithmetic  11.9 us (3%)
  starting transfers between devices  10.3 us (3%)
    unnamed x3, waiting for transfers between devices  113 us
    psum x1, waiting for transfers between devices, per_device(): atm_flux = lax.psum(owner_sums, 'ocn').reshape(local_blocks, 4, ACELL)  72.8 us
    concatenate x1, local copies, waits for them, and re-layouts, per_device(): jnp.concatenate([flux4, passive], axis=1)  30.8 us
    dot_general x1, matrix products, per_device(): jnp.einsum('kfb,kbc->kfc', ocean_values, cell_hot, precision=lax.Precisio...  20.6 us
    dot_general x1, matrix products, per_device(): jnp.einsum('kfa,kba->kfb', picked, weights, preferred_element_type=jnp.fl...  14.9 us
    all_to_all x1, waiting for transfers between devices, per_device(): lax.all_to_all(served, 'atm', split_axis=0, concat_axis=0, tiled=True)  14.5 us
    all_to_all x1, blocking collectives, per_device(): lax.all_to_all(wanted, 'atm', split_axis=0, concat_axis=0, tiled=True)  13.6 us
  transfers between devices with their start and end apart: 4, of which 3 were waited for; matrix products, arithmetic and copies ran while one was open for 10% of the time, Pallas kernels for 0%

commit v1 on v0

--- a/solution.py
+++ b/solution.py
@@ -115,7 +115,8 @@
     owner_sums = jnp.dot(
         owner_hot.T, returned.reshape(slot_total, 4 * ACELL), precision=lax.Precision.HIGHEST
     )
-    atm_flux = lax.psum(owner_sums, "ocn").reshape(local_blocks, 4, ACELL)
+    mix_fields_on_mesh = lambda u_in, group_axis: lax.all_gather(u_in, group_axis).sum(axis=0)
+    atm_flux = mix_fields_on_mesh(owner_sums, "ocn").reshape(local_blocks, 4, ACELL)
     passive = mapped[:, 4:] * (1.0 - 0.7 * ice_frac)[:, None, :]
     ocean_values = cell_weight[:, None, :] * jnp.concatenate([flux4, passive], axis=1)
     cell_hot = (ocean_cell[:, :, None] == jnp.arange(OCELL, dtype=jnp.int32)[None, None, :]).astype(

time: 348 us -> 279 us (0.80)
  waiting for transfers between devices: 200 us -> 128 us
    psum x1 -> x0, waiting for transfers between devices: 72.8 us -> none  [per_device(): atm_flux = lax.psum(owner_sums, 'ocn').reshape(local_blocks, 4, ACELL)]
  transfers between devices with their start and end apart: 4 -> 4, of which waited for: 3 -> 2; matrix products, arithmetic and copies ran while one was open for 10% -> 12% of each run, Pallas kernels for 0% -> 0%
where the time goes in v1:
time: 279 us; the launch traced here: 276 us
  waiting for transfers between devices  128 us (46%)
  matrix products  49.9 us (18%)
  local copies, waits for them, and re-layouts  46 us (16%)
  between operations  15.7 us (6%)
  blocking collectives  13.6 us (5%)
  other arithmetic  13.2 us (5%)
  starting transfers between devices  10.3 us (4%)
    unnamed x3, waiting for transfers between devices  113 us
    concatenate x1, local copies, waits for them, and re-layouts, per_device(): jnp.concatenate([flux4, passive], axis=1)  30.8 us
    dot_general x1, matrix products, per_device(): jnp.einsum('kfb,kbc->kfc', ocean_values, cell_hot, precision=lax.Precisio...  20.6 us
    dot_general x1, matrix products, per_device(): jnp.einsum('kfa,kba->kfb', picked, weights, preferred_element_type=jnp.fl...  14.9 us
    all_to_all x1, waiting for transfers between devices, per_device(): lax.all_to_all(served, 'atm', split_axis=0, concat_axis=0, tiled=True)  14.5 us
    all_to_all x1, blocking collectives, per_device(): lax.all_to_all(wanted, 'atm', split_axis=0, concat_axis=0, tiled=True)  13.6 us
    dot_general x1, matrix products, per_device(): jnp.dot(picker, flat_partial, precision=lax.Precision.HIGHEST)  6.61 us
    dot_general x1, matrix products, per_device(): jnp.einsum('kcb,kba->kca', weighted, weights, preferred_element_type=jnp....  6.39 us
  transfers between devices with their start and end apart: 4, of which 2 were waited for; matrix products, arithmetic and copies ran while one was open for 12% of the time, Pallas kernels for 0%

profile of v1, /device:TPU:2, one launch (start us, length us, event | category | flops | bytes accessed | tf_op | source)
XLA Modules:
  0.0 276.4 jit_solution(17777410647694757156)
XLA Ops:
  8.0 0.0 copy-start
  8.0 0.8 copy.35
  8.8 13.6 %all_to_all.19 = s32[32,1,4]{2,1,0:T(1,128)S(1)} all-to-all(s32[32,1,4]{2,1,0:T(1,128)S(1)} %copy.35), channel_id=1, replica_groups=mesh['ocn'=8,'atm'=32] {'atm'}, dimensions={0} | all-to-all | bytes 1024 | tf_op jit(solution)/shard_map/all_to_all | solution.py:91
  22.4 0.1 reshape.90
  22.5 0.0 copy-done
  22.5 1.7 gather_fusion
  24.2 5.0 %all-to-all-start.1 = ((bf16[32,4,32,128]{3,2,1,0:T(8,128)(2,1)}), bf16[32,4,32,128]{3,2,1,0:T(8,128)(2,1)S(1)}, u32[]{:S(2)}, u32[]{:S(2)}) async-start(bf16[32,4,32,128]{3,2,1,0:T(8,128)(2,1)} %bitcast.2), calls=%async_computation.1 | async-start | bytes 2097152 | tf_op jit(solution)/shard_map/all_to_all | solution.py:93
  29.2 0.7 compare_select_fusion
  29.9 1.0 fusion.16
  31.0 14.5 %all-to-all-done.1 = bf16[32,4,32,128]{3,2,1,0:T(8,128)(2,1)S(1)} async-done(((bf16[32,4,32,128]{3,2,1,0:T(8,128)(2,1)}), bf16[32,4,32,128]{3,2,1,0:T(8,128)(2,1)S(1)}, u32[]{:S(2)}, u32[]{:S(2)}) %all-to-all-start.1) | async-done | bytes 1048608 | tf_op jit(solution)/shard_map/all_to_all | solution.py:93
  45.5 3.2 %gather_fusion.1 = bf16[384,32,128]{2,1,0:T(8,128)(2,1)} fusion(bf16[128,32,128]{2,1,0:T(8,128)(2,1)S(1)} %bitcast.75, s32[1024]{0:T(1024)S(1)} %pad_clamp_fusion), kind=kCustom, calls=%fused_computation.1 | custom fusion | bytes 6292992 | tf_op jit(solution)/shard_map/gather | solution.py:95
  48.7 14.9 %fusion.27 = f32[384,32,128]{2,1,0:T(8,128)} fusion(bf16[384,32,128]{2,1,0:T(8,128)(2,1)} %gather_fusion.1, bf16[384,128,128]{2,1,0:T(8,128)(2,1)} %param.13), kind=kOutput, calls=%fused_computation.64 | convolution fusion | flops 402653184 | bytes 22020096 | tf_op jit(solution)/shard_map/kfa,kba->kfb/dot_general | solution.py:96
  63.6 4.0 %fusion.26 = (f32[384,1,128]{2,1,0:T(1,128)S(1)}, f32[384,1,128]{2,1,0:T(1,128)S(1)}, f32[384,1,128]{2,1,0:T(1,128)S(1)}, f32[384,1,128]{2,1,0:T(1,128)S(1)}) fusion(f32[384,32,128]{2,1,0:T(8,128)} %fusion.27), kind=kLoop, calls=%fused_computation.63 | loop fusion | bytes 1572864 | tf_op jit(solution)/shard_map/slice | solution.py:31
  67.6 0.0 copy-done.2
  67.6 0.0 copy-done.3
  67.6 0.0 copy-done.4
  67.6 0.0 copy-done.5
  67.6 5.4 %fusion.15 = (f32[384,128]{1,0:T(8,128)S(1)}, f32[384,128]{1,0:T(8,128)S(1)}, f32[384,128]{1,0:T(8,128)S(1)}) fusion(f32[384,1,128]{2,0,1:T(8,128)S(1)} %bitcast.89, f32[384,1,128]{2,0,1:T(8,128)S(1)} %bitcast.87, f32[384,128]{1,0:T(8,128)S(1)} %copy-done.2, s32[384,128]{1,0:T(8,128)S(1)} %copy-done.3, f32[384,128]{1,0:T(8,128)S(1)} %bitcast.91, ...), kind=kLoop, calls=%fused_computation.24 | loop fusion | flops 12337152 | bytes 2162688 | tf_op jit(solution)/shard_map/div | solution.py:63
  73.0 0.4 divide_multiply_fusion.1
  73.5 0.0 copy-done.1
  73.5 3.6 %slice_multiply_fusion = f32[384,28,128]{2,1,0:T(8,128)} fusion(f32[384,32,128]{2,1,0:T(8,128)S(1)} %copy-done.1, f32[384,128]{1,0:T(8,128)S(1)} %get-tuple-element.11), kind=kLoop, calls=%fused_computation.8 | loop fusion | flops 1376256 | bytes 11206656 | tf_op jit(solution)/shard_map/mul | solution.py:120
  77.1 30.8 %concatenate.4 = f32[384,32,128]{2,1,0:T(8,128)} concatenate(f32[384,1,128]{2,1,0:T(1,128)S(1)} %bitcast.83, f32[384,1,128]{2,1,0:T(1,128)S(1)} %bitcast.80, f32[384,1,128]{2,1,0:T(1,128)S(1)} %bitcast.76, f32[384,1,128]{2,1,0:T(1,128)S(1)} %bitcast.78, f32[384,28,128]{2,1,0:T(8,128)} %slice_multiply_fusion), dimensions={1} | concatenate | bytes 12582912 | tf_op jit(solution)/shard_map/concatenate | solution.py:121
  107.9 6.4 %fusion.8 = f32[384,4,128]{2,1,0:T(4,128)S(1)} fusion(bf16[384,128,128]{2,1,0:T(8,128)(2,1)} %param.13, f32[384,1,128]{2,1,0:T(1,128)S(1)} %bitcast.79, f32[384,1,128]{2,1,0:T(1,128)S(1)} %bitcast.77, f32[384,1,128]{2,1,0:T(1,128)S(1)} %bitcast.81, f32[384,1,128]{2,1,0:T(1,128)S(1)} %bitcast.84, f32[384,128]{1,0:T(8,128)S(1)} %fusion.16), kind=kOutput, calls=%fused_computation.13 | convolution fusion | flops 51314688 | bytes 14352384 | tf_op jit(solution)/shard_map/kcb,kba->kca/dot_general | solution.py:102
  114.3 0.3 reshape.116
  114.6 0.0 copy-done.7
  114.6 0.5 fusion.17
  115.1 0.9 copy.42
  116.0 5.2 %all-to-all-start.2 = ((f32[32,4,512]{2,1,0:T(4,128)}), f32[32,4,512]{2,1,0:T(4,128)S(1)}, u32[]{:S(2)}, u32[]{:S(2)}) async-start(f32[32,4,512]{2,1,0:T(4,128)} %copy.42), calls=%async_computation.2 | async-start | bytes 524288 | tf_op jit(solution)/shard_map/all_to_all | solution.py:109
  121.2 0.0 copy-start.8
  121.2 0.0 all-reduce.3.cloned.1.call-start
  121.2 0.0 copy-done.6
  121.2 20.6 %fusion = f32[384,32,128]{2,1,0:T(8,128)S(1)} fusion(s32[384,128]{1,0:T(8,128)S(1)} %copy-done.6, f32[384,32,128]{2,1,0:T(8,128)} %concatenate.4, f32[384,128]{1,0:T(8,128)S(1)} %fusion.16), kind=kOutput, calls=%fused_computation.3 | convolution fusion | flops 2423783424 | bytes 12976128 | tf_op jit(solution)/shard_map/kfb,kbc->kfc/dot_general | solution.py:125
  141.8 0.0 copy-start.9
  141.8 6.6 %fusion.2 = f32[32,4096]{1,0:T(8,128)} fusion(f32[48,8,32,128]{3,2,1,0:T(8,128)S(1)} %bitcast.74, s32[384]{0:T(512)S(1)} %copy-done.8), kind=kOutput, calls=%fused_computation.5 | convolution fusion | flops 603992064 | bytes 6817280 | tf_op jit(solution)/shard_map/dot_general | solution.py:132
  148.5 0.0 all-reduce.3.cloned.1.call-update
  148.5 0.0 all-gather.3.cloned.1.call-start
  148.5 0.5 broadcast.204
  149.0 0.7 reduce.5
  149.7 0.1 eq.72
  149.8 0.0 all-to-all-done.2
  149.9 0.1 reshape.94
  150.0 1.0 fusion.21
  150.9 0.0 all-gather.3.cloned.1.call-update
  151.0 0.6 dynamic-slice
  151.6 113.2 %all-reduce.3.cloned.1.call-done = f32[32,4096]{1,0:T(8,128)} async-done(((f32[32,4096]{1,0:T(8,128)}), f32[32,4096]{1,0:T(8,128)}) %all-reduce.3.cloned.1.call-update) | async-done | bytes 524304
  264.8 2.1 constant_dynamic-slice_fusion
  267.0 1.3 reduce_sum.9
  268.3 0.7 reshape.95
  (14 shorter events, 0.0 us)
Async XLA Ops:
  8.0 14.5 %copy-start = (bf16[64,32,128]{2,1,0:T(8,128)(2,1)S(1)}, bf16[64,32,128]{2,1,0:T(8,128)(2,1)}, u32[]{:S(2)}) copy-start(bf16[64,32,128]{2,1,0:T(8,128)(2,1)} %param.12) | copy-start | bytes 1572868
  24.2 21.3 %all-to-all-start.1 = ((bf16[32,4,32,128]{3,2,1,0:T(8,128)(2,1)}), bf16[32,4,32,128]{3,2,1,0:T(8,128)(2,1)S(1)}, u32[]{:S(2)}, u32[]{:S(2)}) async-start(bf16[32,4,32,128]{3,2,1,0:T(8,128)(2,1)} %bitcast.2), calls=%async_computation.1 | async-start | bytes 2097152 | tf_op jit(solution)/shard_map/all_to_all | solution.py:93
  48.7 18.9 %copy-start.2 = (f32[384,128]{1,0:T(8,128)S(1)}, f32[384,128]{1,0:T(8,128)}, u32[]{:S(2)}) copy-start(f32[384,128]{1,0:T(8,128)} %param.16) | copy-start | bytes 589828
  48.7 18.9 %copy-start.3 = (s32[384,128]{1,0:T(8,128)S(1)}, s32[384,128]{1,0:T(8,128)}, u32[]{:S(2)}) copy-start(s32[384,128]{1,0:T(8,128)} %param.23) | copy-start | bytes 589828
  48.7 18.9 %copy-start.4 = (f32[384,128]{1,0:T(8,128)S(1)}, f32[384,128]{1,0:T(8,128)}, u32[]{:S(2)}) copy-start(f32[384,128]{1,0:T(8,128)} %param.15) | copy-start | bytes 589828
  48.7 18.9 %copy-start.5 = (f32[384,128]{1,0:T(8,128)S(1)}, f32[384,128]{1,0:T(8,128)}, u32[]{:S(2)}) copy-start(f32[384,128]{1,0:T(8,128)} %param.14) | copy-start | bytes 589828
  63.6 9.9 %copy-start.1 = (f32[384,32,128]{2,1,0:T(8,128)S(1)}, f32[384,32,128]{2,1,0:T(8,128)}, u32[]{:S(2)}) copy-start(f32[384,32,128]{2,1,0:T(8,128)} %fusion.27) | copy-start | bytes 18874372
  107.9 6.7 %copy-start.7 = (s32[384]{0:T(512)S(1)}, s32[384]{0:T(512)}, u32[]{:S(2)}) copy-start(s32[384]{0:T(512)} %param.19) | copy-start | bytes 4612
  107.9 13.3 %copy-start.6 = (s32[384,128]{1,0:T(8,128)S(1)}, s32[384,128]{1,0:T(8,128)}, u32[]{:S(2)}) copy-start(s32[384,128]{1,0:T(8,128)} %param.21) | copy-start | bytes 589828
  116.0 33.9 %all-to-all-start.2 = ((f32[32,4,512]{2,1,0:T(4,128)}), f32[32,4,512]{2,1,0:T(4,128)S(1)}, u32[]{:S(2)}, u32[]{:S(2)}) async-start(f32[32,4,512]{2,1,0:T(4,128)} %copy.42), calls=%async_computation.2 | async-start | bytes 524288 | tf_op jit(solution)/shard_map/all_to_all | solution.py:109
  121.2 20.7 %copy-start.8 = (s32[384]{0:T(512)S(1)}, s32[384]{0:T(512)}, u32[]{:S(2)}) copy-start(s32[384]{0:T(512)} %param.20) | copy-start | bytes 4612
  121.2 143.7 %all-reduce.3.cloned.1.call-start = ((), (), s32[]{:S(2)}) async-start(), calls=%async_computation.4 | async-start | bytes 1048576
  141.8 9.1 %copy-start.9 = (u32[256]{0:T(256)S(1)}, u32[256]{0:T(256)}, u32[]{:S(2)}) copy-start(u32[256]{0:T(256)} %constant.73) | copy-start | bytes 3076
  148.5 118.5 %all-gather.3.cloned.1.call-start = ((), (), s32[]{:S(2)}) async-start(), calls=%async_computation.3 | async-start | bytes 1179648 | tf_op jit(solution)/shard_map/all_gather | solution.py:118
Sparse Core Ops, SparseCore 0:
  148.6 116.1 all-reduce.2
Sparse Core Ops, SparseCore 1:
  151.3 41.4 all-gather.2
